TPU v7x, 32 devices: a whole 2x2x4 slice. The times are simulated.
32 devices in a mesh: space: 8 (over z, x), blk: 4 (over y, core).
Axes of the slice: x: 2, y: 2, z: 4, core: 2. Of those that a mesh axis runs over, the one named last changes fastest.
Arguments:
- pressure: float32 [512, 16384], P('blk', 'space'), may hold values from -6 to 6
- final_steps: float32 [128, 16384], P(None, 'space'), may hold values from -6 to 6
- weights: float32 [16384], P('space'), may hold values from 0.5 to 4.5, as said below
Outputs:
- spectra: bfloat16 [4, 128, 2, 16384], P(None, 'blk', None, 'space')
- csd: float32 [2, 128, 4, 4], P(None, 'blk')
Inputs may be any that keep to these rules, and one draw needn't show every extreme that they name: Positive weights.
All inputs are finite; a program needn't handle non-finite values.
Results may differ from a plain program's by a relative error of at most 0.0055.
Values may be sent and summed in bfloat16 or wider, within the bound.
A program may use at most 64 MiB of HBM per device.

v0:
```python
import math

import jax
import jax.numpy as jnp
from jax import lax
from jax.sharding import PartitionSpec as P

HOP = 128


def passed_along(value, axis, steps):
    count = lax.axis_size(axis)
    leading, last = (max(0, -steps), min(count, count - steps))
    return lax.ppermute(value, axis, [(source, source + steps) for source in range(leading, last)])


def make_table(blen, nfreq):
    t = jnp.arange(blen, dtype=jnp.int32)
    k = jnp.arange(nfreq, dtype=jnp.int32)
    phase = k[:, None] * t[None, :] % blen
    angle = 2.0 * math.pi / blen * phase.astype(jnp.float32)
    scale = 1.0 / math.sqrt(3.0 * blen / 8.0)
    table = jnp.stack([jnp.cos(angle) * scale, -jnp.sin(angle) * scale], axis=1)
    return table.reshape(2 * nfreq, blen).astype(jnp.bfloat16)


def make_hann(blen):
    t = jnp.arange(blen, dtype=jnp.float32)
    return 0.5 - 0.5 * jnp.cos(2.0 * math.pi / blen * t)


def cross_sums(spectra, weights, count):
    values = spectra.astype(jnp.float32)
    real_part = values[:, :, 0]
    imag_part = values[:, :, 1]
    high = lax.Precision.HIGHEST
    real_w = real_part * weights
    imag_w = imag_part * weights
    first = jnp.einsum("ikn,jkn->kij", real_w, real_part, precision=high) + jnp.einsum(
        "ikn,jkn->kij", imag_w, imag_part, precision=high
    )
    second = jnp.einsum("ikn,jkn->kij", imag_w, real_part, precision=high) - jnp.einsum(
        "ikn,jkn->kij", real_w, imag_part, precision=high
    )
    return jnp.stack([first, second], axis=0) / count


def local(pressure, final_steps, weights):
    blocks_count = lax.axis_size("blk")
    position = lax.axis_index("blk")
    is_last = position == blocks_count - 1
    points = pressure.shape[1]
    own_sum = jnp.sum(pressure, axis=0) + jnp.where(is_last, jnp.sum(final_steps, axis=0), 0.0)
    total = lax.psum(own_sum, "blk")
    mean = total / (HOP * (blocks_count + 1))
    blen = 2 * HOP
    hann = make_hann(blen)
    table = make_table(blen, HOP)
    following = passed_along(pressure, "blk", -1)
    following = jnp.where(is_last, final_steps, following)
    segment = jnp.concatenate([pressure, following], axis=0) - mean
    windowed = (segment * hann[:, None]).astype(jnp.bfloat16)
    coeff = jnp.dot(table, windowed, preferred_element_type=jnp.float32).astype(jnp.bfloat16)
    coeff = coeff.reshape(1, HOP, 2, points)
    spectra = lax.all_to_all(coeff, "blk", split_axis=1, concat_axis=0, tiled=True)
    partial_sums = cross_sums(spectra, weights, float(points * lax.axis_size("space")))
    csd = lax.psum(partial_sums, "space")
    return (spectra, csd)


def solution(mesh):
    return jax.shard_map(
        local,
        mesh=mesh,
        in_specs=(P("blk", "space"), P(None, "space"), P("space")),
        out_specs=(P(None, "blk", None, "space"), P(None, "blk", None, None)),
        check_vma=False,
    )
```

profile of v0, /device:TPU:0, one launch (start us, length us, event | category | flops | bytes accessed | tf_op | source)
XLA Modules:
  0.0 97.0 jit_solution(16759690251978058742)
XLA Ops:
  0.6 1.4 %collective-permute-start = (f32[128,2048]{1,0:T(8,128)}, f32[128,2048]{1,0:T(8,128)S(1)}, u32[]{:S(2)}, u32[]{:S(2)}) collective-permute-start(f32[128,2048]{1,0:T(8,128)} %param.3), channel_id=1, source_target_pairs={{1,0},{2,1},{3,2},{5,4},{6,5},{7,6},{9,8},{10,9},{11,10},{13,12},{... | collective-permute-start | bytes 3145736 | tf_op jit(solution)/shard_map/ppermute | solution.py:14
  2.1 1.3 %reduce_sum.18 = f32[2048]{0:T(1024)S(1)} reduce(f32[128,2048]{1,0:T(8,128)} %param.3, f32[]{:T(128)} %constant.32.clone.1), dimensions={0}, to_apply=%region_0.0 | reduce | flops 260096 | bytes 1056772 | tf_op jit(solution)/shard_map/reduce_sum | solution.py:53
  3.4 0.0 copy-start.1
  3.4 0.5 multiply_convert_fusion
  3.9 0.1 copy.38
  4.1 0.1 convert_element_type.30
  4.2 1.3 %collective-permute-done = f32[128,2048]{1,0:T(8,128)S(1)} collective-permute-done((f32[128,2048]{1,0:T(8,128)}, f32[128,2048]{1,0:T(8,128)S(1)}, u32[]{:S(2)}, u32[]{:S(2)}) %collective-permute-start) | collective-permute-done | bytes 1048608 | tf_op jit(solution)/shard_map/ppermute | solution.py:14
  5.5 1.1 %fusion.23 = (f32[2048]{0:T(1024)S(1)}, f32[128,2048]{1,0:T(8,128)}) fusion(f32[128,2048]{1,0:T(8,128)S(1)} %copy-done, f32[128,2048]{1,0:T(8,128)S(1)} %collective-permute-done, pred[]{:T(512)S(6)} %eq.5), kind=kLoop, calls=%fused_computation.41 | loop fusion | flops 522240 | bytes 3153921 | tf_op jit(solution)/shard_map/reduce_sum | solution.py:53
  6.6 18.7 %psum.14 = f32[2048]{0:T(1024)S(1)} all-reduce(f32[2048]{0:T(1024)S(1)} %select_add_fusion), channel_id=1, replica_groups=mesh['space'=8,'blk'=4] {'blk'}, use_global_device_ids=true, to_apply=%region_2.3 | all-reduce | flops 2048 | bytes 16384 | tf_op jit(solution)/shard_map/psum | solution.py:54
  25.3 1.8 %convolution_convert_fusion = bf16[256,2048]{1,0:T(8,128)(2,1)S(1)} fusion(bf16[256,256]{1,0:T(8,128)(2,1)S(1)} %convert_element_type.30, f32[128,2048]{1,0:T(8,128)} %get-tuple-element.17, f32[128,2048]{1,0:T(8,128)S(1)} %copy-done.1, f32[256]{0:T(256)S(1)} %multiply_subtract_fusion, f32[2048]{0:T(1024)S(1)} %broadcast_multiply_fusion), kind=kOutput, calls=%fused_computation | convolution fusion | flops 271056896 | bytes 3286016 | tf_op jit(solution)/shard_map/dot_general | solution.py:63
  27.1 0.7 reshape.96
  27.8 17.2 %all_to_all.12 = bf16[1,128,2,2048]{3,2,0,1:T(2,128)(2,1)S(1)} all-to-all(bf16[1,128,2,2048]{3,2,0,1:T(2,128)(2,1)S(1)} %bitcast.26), channel_id=1, replica_groups=mesh['space'=8,'blk'=4] {'blk'}, dimensions={1} | all-to-all | bytes 2097152 | tf_op jit(solution)/shard_map/all_to_all | solution.py:65
  45.0 0.3 copy.40
  45.3 0.2 convert_element_type.33
  45.6 0.1 fusion.22
  45.7 2.0 %copy.49 = bf16[4,32,2,2048]{3,2,1,0:T(2,128)(2,1)} copy(bf16[4,32,2,2048]{3,1,0,2:T(8,128)(2,1)S(1)} %bitcast.25) | data formatting | bytes 2097152
  47.7 0.2 fusion.6
  48.0 2.8 %fusion.13 = f32[32,4,4]{2,1,0:T(4,128)S(1)} fusion(f32[4,32,2048]{2,1,0:T(8,128)S(1)} %get-tuple-element.12, bf16[4,32,1,2048]{3,1,0,2:T(8,128)(2,1)S(1)} %get-tuple-element.15), kind=kOutput, calls=%fused_computation.18 | convolution fusion | flops 12582912 | bytes 1574912 | tf_op jit(solution)/shard_map/ikn,jkn->kij/dot_general | solution.py:39
  50.8 2.8 %fusion.9 = f32[32,4,4]{2,1,0:T(4,128)S(1)} fusion(f32[4,32,2048]{2,1,0:T(8,128)S(1)} %get-tuple-element.13, bf16[4,32,1,2048]{3,1,0,2:T(8,128)(2,1)S(1)} %get-tuple-element.15), kind=kOutput, calls=%fused_computation.14 | convolution fusion | flops 12582912 | bytes 1574912 | tf_op jit(solution)/shard_map/ikn,jkn->kij/dot_general | solution.py:42
  53.6 2.4 %fusion.3 = f32[1,32,4,4]{3,2,1,0:T(4,128)S(1)} fusion(f32[32,4,4]{2,1,0:T(4,128)S(1)} %fusion.13, f32[4,32,2048]{2,1,0:T(8,128)S(1)} %get-tuple-element.13, bf16[4,32,1,2048]{3,1,0,2:T(8,128)(2,1)S(1)} %get-tuple-element.14), kind=kOutput, calls=%fused_computation.7 | convolution fusion | flops 12583424 | bytes 1576960 | tf_op jit(solution)/shard_map/ikn,jkn->kij/dot_general | solution.py:39
  56.0 0.1 copy.47
  56.1 2.8 %fusion.2 = f32[1,32,4,4]{3,2,1,0:T(4,128)S(1)} fusion(f32[32,4,4]{2,1,0:T(4,128)S(1)} %fusion.9, f32[4,32,2048]{2,1,0:T(8,128)S(1)} %get-tuple-element.12, bf16[4,32,1,2048]{3,1,0,2:T(8,128)(2,1)S(1)} %get-tuple-element.14), kind=kOutput, calls=%fused_computation.5 | convolution fusion | flops 12583424 | bytes 1576960 | tf_op jit(solution)/shard_map/ikn,jkn->kij/dot_general | solution.py:42
  58.9 0.1 copy.48
  59.0 38.0 %psum.15 = f32[2,32,4,4]{1,3,2,0:T(4,128)} all-reduce(f32[2,32,4,4]{1,3,2,0:T(4,128)S(1)} %maximum_multiply_fusion), channel_id=1, replica_groups=mesh['space'=8,'blk'=4] {'space'}, use_global_device_ids=true, to_apply=%region_3.4 | all-reduce | flops 1024 | bytes 8192 | tf_op jit(solution)/shard_map/psum | solution.py:67
  (10 shorter events, 0.1 us)
Async XLA Ops:
  0.6 4.9 %copy-start = (f32[128,2048]{1,0:T(8,128)S(1)}, f32[128,2048]{1,0:T(8,128)}, u32[]{:S(2)}) copy-start(f32[128,2048]{1,0:T(8,128)} %param.4) | copy-start | bytes 3145732
  0.6 4.9 %collective-permute-start = (f32[128,2048]{1,0:T(8,128)}, f32[128,2048]{1,0:T(8,128)S(1)}, u32[]{:S(2)}, u32[]{:S(2)}) collective-permute-start(f32[128,2048]{1,0:T(8,128)} %param.3), channel_id=1, source_target_pairs={{1,0},{2,1},{3,2},{5,4},{6,5},{7,6},{9,8},{10,9},{11,10},{13,12},{... | collective-permute-start | bytes 3145736 | tf_op jit(solution)/shard_map/ppermute | solution.py:14
  3.4 21.9 %copy-start.1 = (f32[128,2048]{1,0:T(8,128)S(1)}, f32[128,2048]{1,0:T(8,128)}, u32[]{:S(2)}) copy-start(f32[128,2048]{1,0:T(8,128)} %param.3) | copy-start | bytes 3145732
  45.6 2.2 %copy-start.2 = (f32[2048]{0:T(1024)S(1)}, f32[2048]{0:T(1024)}, u32[]{:S(2)}) copy-start(f32[2048]{0:T(1024)} %param.5) | copy-start | bytes 24580
where the time goes:
time: 97.3 us; the launch traced here: 97 us
  blocking collectives  73.8 us (76%)
  matrix products  12.6 us (13%)
  local copies, waits for them, and re-layouts  3.61 us (4%)
  other arithmetic  3.47 us (4%)
  starting transfers between devices  1.42 us (1%)
  waiting for transfers between devices  1.33 us (1%)
    psum x1, blocking collectives, local(): csd = lax.psum(partial_sums, 'space')  38 us
    psum x1, blocking collectives, local(): total = lax.psum(own_sum, 'blk')  18.7 us
    all_to_all x1, blocking collectives, local(): lax.all_to_all(coeff, 'blk', split_axis=1, concat_axis=0, tiled=True)  17.2 us
    dot_general x1, matrix products, cross_sums(): jnp.einsum('ikn,jkn->kij', imag_w, real_part, precision=high)  2.81 us
    dot_general x1, matrix products, cross_sums(): jnp.einsum('ikn,jkn->kij', real_w, imag_part, precision=high)  2.8 us
    dot_general x1, matrix products, cross_sums(): jnp.einsum('ikn,jkn->kij', real_w, real_part, precision=high)  2.79 us
    dot_general x1, matrix products, cross_sums(): jnp.einsum('ikn,jkn->kij', imag_w, imag_part, precision=high)  2.41 us
    unnamed x7, local copies, waits for them, and re-layouts  2.07 us
  transfers between devices with their start and end apart: 1, of which 1 were waited for; matrix products, arithmetic and copies ran while one was open for 2% of the time, Pallas kernels for 0%

commit v1 on v0

v1 whole, which is shorter than its diff:
```python
import functools
import math

import jax
import jax.numpy as jnp
import ml_dtypes
import numpy as np
from jax import lax
from jax.experimental import pallas as pl
from jax.experimental.pallas import tpu as pltpu
from jax.sharding import PartitionSpec as P

HOP = 128
LANES = 128
CHUNKS = 8
MESH = pl.DeviceIdType.MESH


def make_tables(blen, nfreq, groups):
    t = np.arange(blen)
    k = np.arange(nfreq)
    angle = 2.0 * math.pi / blen * (k[:, None] * t[None, :] % blen)
    scale = 1.0 / math.sqrt(3.0 * blen / 8.0)
    table = np.stack([np.cos(angle) * scale, -np.sin(angle) * scale], axis=1)
    table = table.astype(ml_dtypes.bfloat16).astype(np.float64)
    hann = 0.5 - 0.5 * np.cos(2.0 * math.pi / blen * t)
    table = (table * hann).reshape(groups, nfreq // groups, 2, blen)
    split = table.transpose(0, 2, 1, 3).reshape(groups, -1, blen)
    mixed = table.reshape(groups, -1, blen)
    return np.concatenate([split, mixed], axis=1).astype(ml_dtypes.bfloat16)


def each(first, last, body):
    if last - first <= 8:
        for index in range(first, last):
            body(index)
    else:
        pl.loop(first, last)(body)


PAIRS = [(i, j) for i in range(4) for j in range(i, 4)]
CROSS = [(i, j) for i in range(4) for j in range(i + 1, 4)]


def kernel(
    n_space, n_blk, count,
    p_ref, f_ref, w_ref, t_ref, spec_ref, csd_ref,
    p_buf, f_buf, w_buf, t_buf, ranges, sums, x, acc, rows,
    p_sem, f_sem, w_sem, t_sem,
    across_send, across_recv, core_send, core_recv, relay_send, relay_recv,
    sum_send, sum_recv, csd_send, csd_recv,
):
    s, q = lax.axis_index("space"), lax.axis_index("blk")
    width = p_buf.shape[2]
    half = t_buf.shape[0] // 2
    freqs = half // 2
    beside = q + 1 - 2 * (q % 2)
    across = (q + 2) % 4
    diagonal = beside + 2 - 4 * (beside // 2)

    def columns(c):
        return pl.ds(pl.multiple_of(c * width, width), width)

    def load(source, target, sem, c):
        return pltpu.make_async_copy(source.at[:, columns(c)], target.at[c], sem.at[c])

    table_copy = pltpu.make_async_copy(t_ref.at[q], t_buf, t_sem)
    weight_copy = pltpu.make_async_copy(w_ref, w_buf, w_sem)

    barrier = pltpu.get_barrier_semaphore()
    for other in (across, beside, diagonal):
        pl.semaphore_signal(barrier, inc=1, device_id=(s, other), device_id_type=MESH)

    def greet(offset):
        pl.semaphore_signal(barrier, inc=1, device_id=((s + offset) % n_space, q), device_id_type=MESH)

    each(1, n_space, greet)

    for c in range(CHUNKS):
        load(p_ref, p_buf, p_sem, c).start()
    table_copy.start()
    weight_copy.start()
    for c in range(CHUNKS):
        load(f_ref, f_buf, f_sem, c).start()

    def centre(source, target, c, slot):
        values = source[c]
        total = jnp.sum(values, axis=0, keepdims=True)
        sums[slot, :, columns(c)] = total
        target[...] = (values - total * (1.0 / HOP)).astype(jnp.bfloat16)

    @pl.loop(0, CHUNKS)
    def _(c):
        load(p_ref, p_buf, p_sem, c).wait()
        centre(p_buf, ranges.at[c, q], c, q)

    pl.semaphore_wait(barrier, 3 + n_space - 1)

    def send(ref, index, send_sem, recv_sem, other):
        return pltpu.make_async_remote_copy(
            src_ref=ref.at[index], dst_ref=ref.at[index], send_sem=send_sem, recv_sem=recv_sem,
            device_id=(s, other), device_id_type=MESH,
        )

    def sum_copy(which, owner):
        return send(sums, owner, sum_send.at[which], sum_recv.at[which], (across, beside, diagonal)[which])

    def across_copy(c, owner):
        return send(ranges, (c, owner), across_send.at[c], across_recv.at[c], across)

    def core_copy(c, owner):
        return send(ranges, (c, owner), core_send.at[c], core_recv.at[c], beside)

    def relay_copy(c, owner):
        return send(ranges, (c, owner), relay_send.at[c], relay_recv.at[c], beside)

    for which in range(3):
        sum_copy(which, q).start()
    for c in range(CHUNKS):
        across_copy(c, q).start()
    for c in range(CHUNKS):
        core_copy(c, q).start()

    @pl.loop(0, CHUNKS)
    def _(c):
        load(f_ref, f_buf, f_sem, c).wait()
        centre(f_buf, ranges.at[c, n_blk], c, n_blk)

    acc[...] = jnp.zeros_like(acc)
    table_copy.wait()
    weight_copy.wait()
    for which, owner in enumerate((across, beside, diagonal)):
        sum_copy(which, owner).wait_recv()

    def coefficients(c, row):
        table = t_buf[row:row + half, :]
        wide = table.astype(jnp.float32)
        first = jnp.sum(wide[:, :HOP], axis=1, keepdims=True)
        second = jnp.sum(wide[:, HOP:], axis=1, keepdims=True)
        parts = [sums[r, :, columns(c)] for r in range(n_blk + 1)]
        mean = sum(parts[1:], parts[0]) * (1.0 / (HOP * (n_blk + 1)))
        offsets = [part * (1.0 / HOP) - mean for part in parts]
        for b in range(n_blk):
            pair = ranges[c, b:b + 2].reshape(2 * HOP, width)
            value = jnp.dot(table, pair, preferred_element_type=jnp.float32)
            yield b, (value + (first * offsets[b] + second * offsets[b + 1])).astype(jnp.bfloat16)

    def accumulate(c):
        for b, value in coefficients(c, 0):
            x[b] = value.astype(jnp.float32)
        for g in range(freqs // 8):
            low, high = slice(8 * g, 8 * g + 8), slice(freqs + 8 * g, freqs + 8 * g + 8)
            totals = [acc[m, low, :] for m in range(len(PAIRS) + len(CROSS))]
            for tile in range(width // LANES):
                lanes = slice(tile * LANES, (tile + 1) * LANES)
                weight = w_buf[:, pl.ds(pl.multiple_of(c * width + tile * LANES, LANES), LANES)]
                re = [x[b, low, lanes] for b in range(n_blk)]
                im = [x[b, high, lanes] for b in range(n_blk)]
                re_w = [value * weight for value in re]
                im_w = [value * weight for value in im]
                for m, (i, j) in enumerate(PAIRS):
                    totals[m] += re_w[i] * re[j] + im_w[i] * im[j]
                for m, (i, j) in enumerate(CROSS):
                    totals[len(PAIRS) + m] += im_w[i] * re[j] - re_w[i] * im[j]
            for m, total in enumerate(totals):
                acc[m, low, :] = total

    def write(c):
        for b, value in coefficients(c, half):
            spec_ref[b, :, columns(c)] = value

    @pl.loop(0, CHUNKS + 1)
    def _(c):
        @pl.when(c < CHUNKS)
        def _():
            across_copy(c, across).wait_recv()
            relay_copy(c, across).start()

        @pl.when(c > 0)
        def _():
            core_copy(c - 1, beside).wait_recv()
            relay_copy(c - 1, diagonal).wait_recv()
            accumulate(c - 1)

        @pl.when((c > 0) & (c < CHUNKS))
        def _():
            write(c - 1)

    flat = acc[...].reshape(-1, LANES)
    rows[s] = jnp.sum(flat.T, axis=0, keepdims=True)

    def row_copy(offset, owner, peer):
        return pltpu.make_async_remote_copy(
            src_ref=rows.at[owner], dst_ref=rows.at[owner],
            send_sem=csd_send.at[offset], recv_sem=csd_recv.at[owner],
            device_id=(peer, q), device_id_type=MESH,
        )

    each(1, n_space, lambda offset: row_copy(offset, s, (s + offset) % n_space).start())
    write(CHUNKS - 1)

    def arrived(offset):
        peer = (s + offset) % n_space
        row_copy(offset, peer, peer).wait_recv()

    each(1, n_space, arrived)
    csd_ref[...] = jnp.sum(rows[...], axis=0) * (1.0 / count)

    for which in range(3):
        sum_copy(which, q).wait_send()
    for c in range(CHUNKS):
        across_copy(c, q).wait_send()
        core_copy(c, q).wait_send()
        relay_copy(c, across).wait_send()
    each(1, n_space, lambda offset: row_copy(offset, s, (s + offset) % n_space).wait_send())


def local(n_space, n_blk, pressure, final_steps, weights, tables):
    points = pressure.shape[1]
    width = points // CHUNKS
    half = tables.shape[1] // 2
    freqs = half // 2
    kinds = len(PAIRS) + len(CROSS)
    dma = pltpu.SemaphoreType.DMA
    any_space = pl.BlockSpec(memory_space=pl.ANY)
    in_vmem = pl.BlockSpec(memory_space=pltpu.VMEM)
    spectra, row = pl.pallas_call(
        functools.partial(kernel, n_space, n_blk, float(points * n_space)),
        out_shape=(
            jax.ShapeDtypeStruct((n_blk, half, points), jnp.bfloat16),
            jax.ShapeDtypeStruct((1, kinds * freqs), jnp.float32),
        ),
        in_specs=[any_space] * 4,
        out_specs=(in_vmem, in_vmem),
        scratch_shapes=[
            pltpu.VMEM((CHUNKS, HOP, width), jnp.float32),
            pltpu.VMEM((CHUNKS, HOP, width), jnp.float32),
            pltpu.VMEM((1, points), jnp.float32),
            pltpu.VMEM(tables.shape[1:], jnp.bfloat16),
            pltpu.VMEM((CHUNKS, n_blk + 1, HOP, width), jnp.bfloat16),
            pltpu.VMEM((n_blk + 1, 1, points), jnp.float32),
            pltpu.VMEM((n_blk, half, width), jnp.float32),
            pltpu.VMEM((kinds, freqs, LANES), jnp.float32),
            pltpu.VMEM((n_space, 1, kinds * freqs), jnp.float32),
            dma((CHUNKS,)), dma((CHUNKS,)), dma(()), dma(()),
            dma((CHUNKS,)), dma((CHUNKS,)), dma((CHUNKS,)), dma((CHUNKS,)), dma((CHUNKS,)), dma((CHUNKS,)),
            dma((3,)), dma((3,)), dma((n_space,)), dma((n_space,)),
        ],
        compiler_params=pltpu.CompilerParams(
            collective_id=0, has_side_effects=True, vmem_limit_bytes=32 * 1024 * 1024
        ),
    )(pressure, final_steps, weights.reshape(1, points), tables)
    spectra = spectra.reshape(n_blk, freqs, 2, points)
    row = row.reshape(kinds, freqs)
    zero = jnp.zeros_like(row[0])
    full = []
    for i in range(4):
        for j in range(4):
            full.append(row[PAIRS.index((min(i, j), max(i, j)))])
    for i in range(4):
        for j in range(4):
            at = len(PAIRS) + CROSS.index((min(i, j), max(i, j))) if i != j else 0
            full.append(zero if i == j else row[at] if i < j else -row[at])
    csd = jnp.stack(full).reshape(2, 4, 4, freqs).transpose(0, 3, 1, 2)
    return spectra, csd


def solution(mesh):
    n_space, n_blk = mesh.shape["space"], mesh.shape["blk"]
    tables = make_tables(2 * HOP, HOP, n_blk)
    mapped = jax.shard_map(
        functools.partial(local, n_space, n_blk),
        mesh=mesh,
        in_specs=(P("blk", "space"), P(None, "space"), P("space"), P()),
        out_specs=(P(None, "blk", None, "space"), P(None, "blk", None, None)),
        check_vma=False,
    )

    def run(pressure, final_steps, weights):
        return mapped(pressure, final_steps, weights, jnp.asarray(tables))

    return run
```

time: 97.3 us -> 33 us (0.34)
  blocking collectives: 73.8 us -> 0 us
  Pallas kernels: 0 us -> 23.9 us
  matrix products: 12.6 us -> 0 us
  local copies, waits for them, and re-layouts: 3.61 us -> 8.1 us
  other arithmetic: 3.47 us -> 0.07 us
  starting transfers between devices: 1.42 us -> 0 us
  waiting for transfers between devices: 1.33 us -> 0 us
    psum x2 -> x0, blocking collectives: 56.6 us -> none  [the longest x1 38 us: local(): csd = lax.psum(partial_sums, 'space')]
    pallas_call x0 -> x1, Pallas kernels: none -> 23.9 us  [local(): pl.pallas_call(functools.partial(kernel, n_space, n_blk, float(points * n...]
    all_to_all x1 -> x0, blocking collectives: 17.2 us -> none  [local(): lax.all_to_all(coeff, 'blk', split_axis=1, concat_axis=0, tiled=True)]
    dot_general x5 -> x0, matrix products: 12.6 us -> none  [the longest x1 2.81 us: cross_sums(): jnp.einsum('ikn,jkn->kij', imag_w, real_part, precision=high)]
    reduce_sum x2 -> x0, other arithmetic: 2.38 us -> none  [the longest x1 1.29 us: local(): jnp.sum(pressure, axis=0)]
    another operation x3 -> x2, local copies, waits for them, and re-layouts: 0.34 us -> 2.44 us  [the longest x1 2.44 us: local(): csd = jnp.stack(full).reshape(2, 4, 4, freqs).transpose(0, 3, 1, 2)]
    unnamed x7 -> x8, local copies, waits for them, and re-layouts: 2.07 us -> 4.09 us
    ppermute x1 -> x0, starting transfers between devices: 1.42 us -> none  [passed_along(): lax.ppermute(value, axis, [(source, source + steps) for source in range(l...]
  transfers between devices with their start and end apart: 1 -> 0, of which waited for: 1 -> 0; matrix products, arithmetic and copies ran while one was open for 2% -> 0% of each run, Pallas kernels for 0% -> 0%
where the time goes in v1:
time: 33 us; the launch traced here: 32.8 us
  Pallas kernels  23.9 us (72%)
  local copies, waits for them, and re-layouts  8.1 us (25%)
  between operations  0.65 us (2%)
    pallas_call x1, Pallas kernels, local(): pl.pallas_call(functools.partial(kernel, n_space, n_blk, float(points * n...  23.9 us
    unnamed x8, local copies, waits for them, and re-layouts  4.09 us
    another operation x1, local copies, waits for them, and re-layouts, local(): csd = jnp.stack(full).reshape(2, 4, 4, freqs).transpose(0, 3, 1, 2)  2.44 us
    reshape x1, local copies, waits for them, and re-layouts, local(): spectra = spectra.reshape(n_blk, freqs, 2, points)  1.5 us

profile of v1, /device:TPU:0, one launch (start us, length us, event | category | flops | bytes accessed | tf_op | source)
XLA Modules:
  0.0 32.8 jit_solution(18196778673609146102)
XLA Ops:
  0.6 0.0 copy-start
  0.6 1.2 %copy-done = f32[128,2048]{1,0:T(8,128)S(1)} copy-done((f32[128,2048]{1,0:T(8,128)S(1)}, f32[128,2048]{1,0:T(8,128)}, u32[]{:S(2)}) %copy-start) | copy-done | bytes 1048600
  1.9 0.0 copy-start.1
  1.9 1.2 %copy-done.1 = f32[128,2048]{1,0:T(8,128)S(1)} copy-done((f32[128,2048]{1,0:T(8,128)S(1)}, f32[128,2048]{1,0:T(8,128)}, u32[]{:S(2)}) %copy-start.1) | copy-done | bytes 1048600
  3.1 0.0 copy-start.2
  3.1 0.9 %copy-done.2 = bf16[4,128,256]{2,1,0:T(8,128)(2,1)S(1)} copy-done((bf16[4,128,256]{2,1,0:T(8,128)(2,1)S(1)}, bf16[4,128,256]{2,1,0:T(8,128)(2,1)}, u32[]{:S(2)}) %copy-start.2) | copy-done | bytes 262168
  4.0 0.0 copy-start.3
  4.0 0.7 %copy-done.3 = f32[2048]{0:T(1024)S(1)} copy-done((f32[2048]{0:T(1024)S(1)}, f32[2048]{0:T(1024)}, u32[]{:S(2)}) %copy-start.3) | copy-done | bytes 8216
  4.7 23.9 %shard_map.59 = (bf16[4,64,2048]{2,1,0:T(8,128)(2,1)S(1)}, f32[1,512]{1,0:T(1,128)S(1)}) custom-call(f32[128,2048]{1,0:T(8,128)S(1)} %copy-done, f32[128,2048]{1,0:T(8,128)S(1)} %copy-done.1, f32[1,2048]{1,0:T(1,128)S(1)} %bitcast.4, bf16[4,128,256]{2,1,0:T(8,128)(2,1)S(1)} %copy-done.2), custom_call_target="tpu_custom_call" | custom-call | tf_op jit(solution)/shard_map/pallas_call | solution.py:227
  28.7 1.5 %reshape.31 = bf16[4,32,2,2048]{3,2,1,0:T(2,128)(2,1)} reshape(bf16[4,64,2048]{2,1,0:T(8,128)(2,1)S(1)} %get-tuple-element.4) | data formatting | bytes 2097152 | tf_op jit(solution)/shard_map/reshape | solution.py:253
  30.2 0.1 fusion
  30.3 0.1 slice_negate_fusion
  30.3 2.4 %stack.2 = f32[32,32]{1,0:T(8,128)} concatenate(f32[1,32]{1,0:T(1,128)S(1)} %get-tuple-element.27, f32[1,32]{1,0:T(1,128)S(1)} %get-tuple-element.26, f32[1,32]{1,0:T(1,128)S(1)} %get-tuple-element.25, f32[1,32]{1,0:T(1,128)S(1)} %get-tuple-element.24, f32[1,32]{1,0:T(1,128)S(1)} %get-tuple-element.26, f32[1,32]{1,0:T(1,128)S(1)} %get-tuple-element.23, ...), dimensions={0} | concatenate | bytes 8192 | tf_op jit(solution)/shard_map/stack | solution.py:264
  (1 shorter events, 0.0 us)
Async XLA Ops:
  0.6 1.2 %copy-start = (f32[128,2048]{1,0:T(8,128)S(1)}, f32[128,2048]{1,0:T(8,128)}, u32[]{:S(2)}) copy-start(f32[128,2048]{1,0:T(8,128)} %p_ref.1) | copy-start | bytes 3145732
  1.9 1.2 %copy-start.1 = (f32[128,2048]{1,0:T(8,128)S(1)}, f32[128,2048]{1,0:T(8,128)}, u32[]{:S(2)}) copy-start(f32[128,2048]{1,0:T(8,128)} %f_ref.1) | copy-start | bytes 3145732
  3.1 0.9 %copy-start.2 = (bf16[4,128,256]{2,1,0:T(8,128)(2,1)S(1)}, bf16[4,128,256]{2,1,0:T(8,128)(2,1)}, u32[]{:S(2)}) copy-start(bf16[4,128,256]{2,1,0:T(8,128)(2,1)} %constant.4.clone.t_ref) | copy-start | bytes 786436
  4.0 0.7 %copy-start.3 = (f32[2048]{0:T(1024)S(1)}, f32[2048]{0:T(1024)}, u32[]{:S(2)}) copy-start(f32[2048]{0:T(1024)} %param.6) | copy-start | bytes 24580

commit v2 on v1

--- a/solution.py
+++ b/solution.py
@@ -89,13 +89,6 @@
         sums[slot, :, columns(c)] = total
         target[...] = (values - total * (1.0 / HOP)).astype(jnp.bfloat16)
 
-    @pl.loop(0, CHUNKS)
-    def _(c):
-        load(p_ref, p_buf, p_sem, c).wait()
-        centre(p_buf, ranges.at[c, q], c, q)
-
-    pl.semaphore_wait(barrier, 3 + n_space - 1)
-
     def send(ref, index, send_sem, recv_sem, other):
         return pltpu.make_async_remote_copy(
             src_ref=ref.at[index], dst_ref=ref.at[index], send_sem=send_sem, recv_sem=recv_sem,
@@ -114,12 +107,24 @@
     def relay_copy(c, owner):
         return send(ranges, (c, owner), relay_send.at[c], relay_recv.at[c], beside)
 
+    def prepare(c):
+        load(p_ref, p_buf, p_sem, c).wait()
+        centre(p_buf, ranges.at[c, q], c, q)
+
+    def share(c):
+        across_copy(c, q).start()
+        core_copy(c, q).start()
+
+    prepare(0)
+    pl.semaphore_wait(barrier, 3 + n_space - 1)
+    share(0)
+    prepare(1)
+    share(1)
+    pl.loop(2, CHUNKS)(prepare)
     for which in range(3):
         sum_copy(which, q).start()
-    for c in range(CHUNKS):
-        across_copy(c, q).start()
-    for c in range(CHUNKS):
-        core_copy(c, q).start()
+    for c in range(2, CHUNKS):
+        share(c)
 
     @pl.loop(0, CHUNKS)
     def _(c):
@@ -167,7 +172,7 @@
 
     def write(c):
         for b, value in coefficients(c, half):
-            spec_ref[b, :, columns(c)] = value
+            spec_ref[b, :, :, columns(c)] = value.reshape(freqs, 2, width)
 
     @pl.loop(0, CHUNKS + 1)
     def _(c):
@@ -204,7 +209,16 @@
         row_copy(offset, peer, peer).wait_recv()
 
     each(1, n_space, arrived)
-    csd_ref[...] = jnp.sum(rows[...], axis=0) * (1.0 / count)
+    total = jnp.sum(rows[...], axis=0) * (1.0 / count)
+    csd_ref[...] = jnp.zeros_like(csd_ref)
+    for m, (i, j) in enumerate(PAIRS + CROSS):
+        line = total[:, m * freqs:(m + 1) * freqs]
+        if m < len(PAIRS):
+            for row in {4 * i + j, 4 * j + i}:
+                csd_ref[row:row + 1, :] = line
+        else:
+            csd_ref[16 + 4 * i + j:17 + 4 * i + j, :] = line
+            csd_ref[16 + 4 * j + i:17 + 4 * j + i, :] = -line
 
     for which in range(3):
         sum_copy(which, q).wait_send()
@@ -222,15 +236,15 @@
     freqs = half // 2
     kinds = len(PAIRS) + len(CROSS)
     dma = pltpu.SemaphoreType.DMA
-    any_space = pl.BlockSpec(memory_space=pl.ANY)
+    in_hbm = pl.BlockSpec(memory_space=pltpu.HBM)
     in_vmem = pl.BlockSpec(memory_space=pltpu.VMEM)
-    spectra, row = pl.pallas_call(
+    spectra, csd = pl.pallas_call(
         functools.partial(kernel, n_space, n_blk, float(points * n_space)),
         out_shape=(
-            jax.ShapeDtypeStruct((n_blk, half, points), jnp.bfloat16),
-            jax.ShapeDtypeStruct((1, kinds * freqs), jnp.float32),
+            jax.ShapeDtypeStruct((n_blk, freqs, 2, points), jnp.bfloat16),
+            jax.ShapeDtypeStruct((32, freqs), jnp.float32),
         ),
-        in_specs=[any_space] * 4,
+        in_specs=[in_hbm] * 4,
         out_specs=(in_vmem, in_vmem),
         scratch_shapes=[
             pltpu.VMEM((CHUNKS, HOP, width), jnp.float32),
@@ -247,21 +261,10 @@
             dma((3,)), dma((3,)), dma((n_space,)), dma((n_space,)),
         ],
         compiler_params=pltpu.CompilerParams(
-            collective_id=0, has_side_effects=True, vmem_limit_bytes=32 * 1024 * 1024
+            collective_id=0, has_side_effects=True, vmem_limit_bytes=52 * 1024 * 1024
         ),
     )(pressure, final_steps, weights.reshape(1, points), tables)
-    spectra = spectra.reshape(n_blk, freqs, 2, points)
-    row = row.reshape(kinds, freqs)
-    zero = jnp.zeros_like(row[0])
-    full = []
-    for i in range(4):
-        for j in range(4):
-            full.append(row[PAIRS.index((min(i, j), max(i, j)))])
-    for i in range(4):
-        for j in range(4):
-            at = len(PAIRS) + CROSS.index((min(i, j), max(i, j))) if i != j else 0
-            full.append(zero if i == j else row[at] if i < j else -row[at])
-    csd = jnp.stack(full).reshape(2, 4, 4, freqs).transpose(0, 3, 1, 2)
+    csd = csd.reshape(2, 4, 4, freqs).transpose(0, 3, 1, 2)
     return spectra, csd
 
 

time: 33 us -> 28.2 us (0.85)
  local copies, waits for them, and re-layouts: 8.1 us -> 3.22 us
    another operation x2 -> x0, local copies, waits for them, and re-layouts: 2.44 us -> none  [the longest x1 2.44 us: local(): csd = jnp.stack(full).reshape(2, 4, 4, freqs).transpose(0, 3, 1, 2)]
    reshape x1 -> x0, local copies, waits for them, and re-layouts: 1.5 us -> none  [local(): spectra = spectra.reshape(n_blk, freqs, 2, points)]
    unnamed x8 -> x6, local copies, waits for them, and re-layouts: 4.09 us -> 3.22 us
where the time goes in v2:
time: 28.2 us; the launch traced here: 28 us
  Pallas kernels  24.2 us (86%)
  local copies, waits for them, and re-layouts  3.22 us (11%)
  between operations  0.65 us (2%)
    pallas_call x1, Pallas kernels, local(): pl.pallas_call(functools.partial(kernel, n_space, n_blk, float(points * n...  24.2 us
    unnamed x6, local copies, waits for them, and re-layouts  3.22 us

profile of v2, /device:TPU:0, one launch (start us, length us, event | category | flops | bytes accessed | tf_op | source)
XLA Modules:
  0.0 28.0 jit_solution(4435688747177435323)
XLA Ops:
  0.6 0.0 copy-start
  0.6 0.9 %copy-done = bf16[4,128,256]{2,1,0:T(8,128)(2,1)S(1)} copy-done((bf16[4,128,256]{2,1,0:T(8,128)(2,1)S(1)}, bf16[4,128,256]{2,1,0:T(8,128)(2,1)}, u32[]{:S(2)}) %copy-start) | copy-done | bytes 262168
  1.6 0.0 copy-start.1
  1.6 0.7 %copy-done.1 = f32[2048]{0:T(1024)S(1)} copy-done((f32[2048]{0:T(1024)S(1)}, f32[2048]{0:T(1024)}, u32[]{:S(2)}) %copy-start.1) | copy-done | bytes 8216
  2.3 24.2 %shard_map.59 = (bf16[4,32,2,2048]{3,2,1,0:T(2,128)(2,1)S(1)}, f32[32,32]{1,0:T(8,128)S(1)}) custom-call(f32[128,2048]{1,0:T(8,128)} %p_ref.1, f32[128,2048]{1,0:T(8,128)} %f_ref.1, f32[1,2048]{1,0:T(1,128)S(1)} %bitcast.5, bf16[4,128,256]{2,1,0:T(8,128)(2,1)S(1)} %copy-done), custom_call_target="tpu_custom_call" | custom-call | tf_op jit(solution)/shard_map/pallas_call | solution.py:241
  26.4 1.0 %copy.8 = bf16[4,32,2,2048]{3,2,1,0:T(2,128)(2,1)} copy(bf16[4,32,2,2048]{3,2,1,0:T(2,128)(2,1)S(1)} %get-tuple-element.8) | data formatting | bytes 2097152
  27.4 0.6 %copy.9 = f32[2,32,4,4]{1,3,2,0:T(4,128)} copy(f32[2,32,4,4]{1,3,2,0:T(4,128)S(1)} %bitcast.4) | data formatting | bytes 8192
Async XLA Ops:
  0.6 1.0 %copy-start = (bf16[4,128,256]{2,1,0:T(8,128)(2,1)S(1)}, bf16[4,128,256]{2,1,0:T(8,128)(2,1)}, u32[]{:S(2)}) copy-start(bf16[4,128,256]{2,1,0:T(8,128)(2,1)} %constant.2.clone.t_ref) | copy-start | bytes 786436
  1.6 0.7 %copy-start.1 = (f32[2048]{0:T(1024)S(1)}, f32[2048]{0:T(1024)}, u32[]{:S(2)}) copy-start(f32[2048]{0:T(1024)} %param.6) | copy-start | bytes 24580

commit v3 on v2

--- a/solution.py
+++ b/solution.py
@@ -3,8 +3,6 @@
 
 import jax
 import jax.numpy as jnp
-import ml_dtypes
-import numpy as np
 from jax import lax
 from jax.experimental import pallas as pl
 from jax.experimental.pallas import tpu as pltpu
@@ -16,18 +14,19 @@
 MESH = pl.DeviceIdType.MESH
 
 
-def make_tables(blen, nfreq, groups):
-    t = np.arange(blen)
-    k = np.arange(nfreq)
-    angle = 2.0 * math.pi / blen * (k[:, None] * t[None, :] % blen)
-    scale = 1.0 / math.sqrt(3.0 * blen / 8.0)
-    table = np.stack([np.cos(angle) * scale, -np.sin(angle) * scale], axis=1)
-    table = table.astype(ml_dtypes.bfloat16).astype(np.float64)
-    hann = 0.5 - 0.5 * np.cos(2.0 * math.pi / blen * t)
-    table = (table * hann).reshape(groups, nfreq // groups, 2, blen)
-    split = table.transpose(0, 2, 1, 3).reshape(groups, -1, blen)
-    mixed = table.reshape(groups, -1, blen)
-    return np.concatenate([split, mixed], axis=1).astype(ml_dtypes.bfloat16)
+def make_table(rows, freqs, group):
+    blen = 2 * HOP
+    row = lax.broadcasted_iota(jnp.int32, (rows, blen), 0)
+    t = lax.broadcasted_iota(jnp.int32, (rows, blen), 1)
+    mixed = row >= 2 * freqs
+    inner = jnp.where(mixed, row - 2 * freqs, row)
+    k = group * freqs + jnp.where(mixed, lax.div(inner, 2), lax.rem(inner, freqs))
+    part = jnp.where(mixed, lax.rem(inner, 2), lax.div(inner, freqs))
+    step = 2.0 * math.pi / blen
+    phase = lax.rem(k * t + part * (blen // 4), blen)
+    table = jnp.cos(phase.astype(jnp.float32) * step) * (1.0 / math.sqrt(3.0 * blen / 8.0))
+    hann = 0.5 - 0.5 * jnp.cos(t[:8].astype(jnp.float32) * step)
+    return table.astype(jnp.bfloat16).astype(jnp.float32) * hann[:1]
 
 
 def each(first, last, body):
@@ -44,9 +43,9 @@
 
 def kernel(
     n_space, n_blk, count,
-    p_ref, f_ref, w_ref, t_ref, spec_ref, csd_ref,
-    p_buf, f_buf, w_buf, t_buf, ranges, sums, x, acc, rows,
-    p_sem, f_sem, w_sem, t_sem,
+    p_ref, f_ref, w_ref, spec_ref, csd_ref,
+    p_buf, f_buf, w_buf, t_buf, edges, ranges, sums, x, acc, rows,
+    p_sem, f_sem, w_sem,
     across_send, across_recv, core_send, core_recv, relay_send, relay_recv,
     sum_send, sum_recv, csd_send, csd_recv,
 ):
@@ -64,7 +63,6 @@
     def load(source, target, sem, c):
         return pltpu.make_async_copy(source.at[:, columns(c)], target.at[c], sem.at[c])
 
-    table_copy = pltpu.make_async_copy(t_ref.at[q], t_buf, t_sem)
     weight_copy = pltpu.make_async_copy(w_ref, w_buf, w_sem)
 
     barrier = pltpu.get_barrier_semaphore()
@@ -78,7 +76,6 @@
 
     for c in range(CHUNKS):
         load(p_ref, p_buf, p_sem, c).start()
-    table_copy.start()
     weight_copy.start()
     for c in range(CHUNKS):
         load(f_ref, f_buf, f_sem, c).start()
@@ -132,27 +129,32 @@
         centre(f_buf, ranges.at[c, n_blk], c, n_blk)
 
     acc[...] = jnp.zeros_like(acc)
-    table_copy.wait()
+    table = make_table(2 * half, freqs, q)
+    t_buf[...] = table.astype(jnp.bfloat16)
+    for side in range(2):
+        total = jnp.sum(table[:, side * HOP:(side + 1) * HOP], axis=1, keepdims=True)
+        edges[side] = jnp.broadcast_to(total, edges.shape[1:])
     weight_copy.wait()
     for which, owner in enumerate((across, beside, diagonal)):
         sum_copy(which, owner).wait_recv()
 
-    def coefficients(c, row):
-        table = t_buf[row:row + half, :]
-        wide = table.astype(jnp.float32)
-        first = jnp.sum(wide[:, :HOP], axis=1, keepdims=True)
-        second = jnp.sum(wide[:, HOP:], axis=1, keepdims=True)
+    def coefficients(c, first, last):
+        before, after = (jnp.tile(edges[side, first:last, :], (1, width // LANES)) for side in range(2))
         parts = [sums[r, :, columns(c)] for r in range(n_blk + 1)]
         mean = sum(parts[1:], parts[0]) * (1.0 / (HOP * (n_blk + 1)))
         offsets = [part * (1.0 / HOP) - mean for part in parts]
         for b in range(n_blk):
             pair = ranges[c, b:b + 2].reshape(2 * HOP, width)
-            value = jnp.dot(table, pair, preferred_element_type=jnp.float32)
-            yield b, (value + (first * offsets[b] + second * offsets[b + 1])).astype(jnp.bfloat16)
+            value = jnp.dot(t_buf[first:last, :], pair, preferred_element_type=jnp.float32)
+            yield b, (value + (before * offsets[b] + after * offsets[b + 1])).astype(jnp.bfloat16)
+
+    def keep(b, value):
+        x[b] = value.astype(jnp.float32)
+
+    def write(c, b, value):
+        spec_ref[b, :, :, columns(c)] = value.reshape(freqs, 2, width)
 
     def accumulate(c):
-        for b, value in coefficients(c, 0):
-            x[b] = value.astype(jnp.float32)
         for g in range(freqs // 8):
             low, high = slice(8 * g, 8 * g + 8), slice(freqs + 8 * g, freqs + 8 * g + 8)
             totals = [acc[m, low, :] for m in range(len(PAIRS) + len(CROSS))]
@@ -170,26 +172,29 @@
             for m, total in enumerate(totals):
                 acc[m, low, :] = total
 
-    def write(c):
-        for b, value in coefficients(c, half):
-            spec_ref[b, :, :, columns(c)] = value.reshape(freqs, 2, width)
-
-    @pl.loop(0, CHUNKS + 1)
+    def receive(c):
+        across_copy(c, across).wait_recv()
+        relay_copy(c, across).start()
+
+    def receive_relayed(c):
+        core_copy(c, beside).wait_recv()
+        relay_copy(c, diagonal).wait_recv()
+
+    receive(0)
+
+    @pl.loop(1, CHUNKS)
     def _(c):
-        @pl.when(c < CHUNKS)
-        def _():
-            across_copy(c, across).wait_recv()
-            relay_copy(c, across).start()
-
-        @pl.when(c > 0)
-        def _():
-            core_copy(c - 1, beside).wait_recv()
-            relay_copy(c - 1, diagonal).wait_recv()
-            accumulate(c - 1)
-
-        @pl.when((c > 0) & (c < CHUNKS))
-        def _():
-            write(c - 1)
+        receive(c)
+        receive_relayed(c - 1)
+        for b, value in coefficients(c - 1, 0, 2 * half):
+            keep(b, value[:half])
+            write(c - 1, b, value[half:])
+        accumulate(c - 1)
+
+    receive_relayed(CHUNKS - 1)
+    for b, value in coefficients(CHUNKS - 1, 0, half):
+        keep(b, value)
+    accumulate(CHUNKS - 1)
 
     flat = acc[...].reshape(-1, LANES)
     rows[s] = jnp.sum(flat.T, axis=0, keepdims=True)
@@ -202,7 +207,8 @@
         )
 
     each(1, n_space, lambda offset: row_copy(offset, s, (s + offset) % n_space).start())
-    write(CHUNKS - 1)
+    for b, value in coefficients(CHUNKS - 1, half, 2 * half):
+        write(CHUNKS - 1, b, value)
 
     def arrived(offset):
         peer = (s + offset) % n_space
@@ -229,11 +235,22 @@
     each(1, n_space, lambda offset: row_copy(offset, s, (s + offset) % n_space).wait_send())
 
 
-def local(n_space, n_blk, pressure, final_steps, weights, tables):
+def finish(spec_ref, csd_ref, spec_out, csd_out, sems):
+    copies = [
+        pltpu.make_async_copy(spec_ref, spec_out, sems.at[0]),
+        pltpu.make_async_copy(csd_ref, csd_out, sems.at[1]),
+    ]
+    for copy in copies:
+        copy.start()
+    for copy in copies:
+        copy.wait()
+
+
+def local(n_space, n_blk, pressure, final_steps, weights):
     points = pressure.shape[1]
     width = points // CHUNKS
-    half = tables.shape[1] // 2
-    freqs = half // 2
+    freqs = HOP // n_blk
+    half = 2 * freqs
     kinds = len(PAIRS) + len(CROSS)
     dma = pltpu.SemaphoreType.DMA
     in_hbm = pl.BlockSpec(memory_space=pltpu.HBM)
@@ -244,42 +261,48 @@
             jax.ShapeDtypeStruct((n_blk, freqs, 2, points), jnp.bfloat16),
             jax.ShapeDtypeStruct((32, freqs), jnp.float32),
         ),
-        in_specs=[in_hbm] * 4,
+        in_specs=[in_hbm] * 3,
         out_specs=(in_vmem, in_vmem),
         scratch_shapes=[
             pltpu.VMEM((CHUNKS, HOP, width), jnp.float32),
             pltpu.VMEM((CHUNKS, HOP, width), jnp.float32),
             pltpu.VMEM((1, points), jnp.float32),
-            pltpu.VMEM(tables.shape[1:], jnp.bfloat16),
+            pltpu.VMEM((2 * half, 2 * HOP), jnp.bfloat16),
+            pltpu.VMEM((2, 2 * half, LANES), jnp.float32),
             pltpu.VMEM((CHUNKS, n_blk + 1, HOP, width), jnp.bfloat16),
             pltpu.VMEM((n_blk + 1, 1, points), jnp.float32),
             pltpu.VMEM((n_blk, half, width), jnp.float32),
             pltpu.VMEM((kinds, freqs, LANES), jnp.float32),
             pltpu.VMEM((n_space, 1, kinds * freqs), jnp.float32),
-            dma((CHUNKS,)), dma((CHUNKS,)), dma(()), dma(()),
+            dma((CHUNKS,)), dma((CHUNKS,)), dma(()),
             dma((CHUNKS,)), dma((CHUNKS,)), dma((CHUNKS,)), dma((CHUNKS,)), dma((CHUNKS,)), dma((CHUNKS,)),
             dma((3,)), dma((3,)), dma((n_space,)), dma((n_space,)),
         ],
         compiler_params=pltpu.CompilerParams(
             collective_id=0, has_side_effects=True, vmem_limit_bytes=52 * 1024 * 1024
         ),
-    )(pressure, final_steps, weights.reshape(1, points), tables)
+    )(pressure, final_steps, weights.reshape(1, points))
+    spectra, csd = pl.pallas_call(
+        finish,
+        out_shape=(
+            jax.ShapeDtypeStruct(spectra.shape, spectra.dtype),
+            jax.ShapeDtypeStruct(csd.shape, csd.dtype),
+        ),
+        in_specs=[pl.BlockSpec(memory_space=pl.ANY)] * 2,
+        out_specs=(in_hbm, in_hbm),
+        scratch_shapes=[dma((2,))],
+        compiler_params=pltpu.CompilerParams(vmem_limit_bytes=1024 * 1024),
+    )(spectra, csd)
     csd = csd.reshape(2, 4, 4, freqs).transpose(0, 3, 1, 2)
     return spectra, csd
 
 
 def solution(mesh):
     n_space, n_blk = mesh.shape["space"], mesh.shape["blk"]
-    tables = make_tables(2 * HOP, HOP, n_blk)
-    mapped = jax.shard_map(
+    return jax.shard_map(
         functools.partial(local, n_space, n_blk),
         mesh=mesh,
-        in_specs=(P("blk", "space"), P(None, "space"), P("space"), P()),
+        in_specs=(P("blk", "space"), P(None, "space"), P("space")),
         out_specs=(P(None, "blk", None, "space"), P(None, "blk", None, None)),
         check_vma=False,
     )
-
-    def run(pressure, final_steps, weights):
-        return mapped(pressure, final_steps, weights, jnp.asarray(tables))
-
-    return run

time: 28.2 us -> 26.5 us (0.940)
  local copies, waits for them, and re-layouts: 3.22 us -> 0.69 us
  Pallas kernels: 24.2 us -> 24.9 us
    unnamed x6 -> x2, local copies, waits for them, and re-layouts: 3.22 us -> 0.69 us
    pallas_call x0 -> x1, Pallas kernels: none -> 0.99 us  [local(): pl.pallas_call(finish, out_shape=(jax.ShapeDtypeStruct(spectra.shape, spe...]
where the time goes in v3:
time: 26.5 us; the launch traced here: 26.3 us
  Pallas kernels  24.9 us (94%)
  local copies, waits for them, and re-layouts  0.69 us (3%)
  between operations  0.65 us (2%)
    pallas_call x1, Pallas kernels, local(): pl.pallas_call(functools.partial(kernel, n_space, n_blk, float(points * n...  23.9 us
    pallas_call x1, Pallas kernels, local(): pl.pallas_call(finish, out_shape=(jax.ShapeDtypeStruct(spectra.shape, spe...  0.99 us
    unnamed x2, local copies, waits for them, and re-layouts  0.69 us

profile of v3, /device:TPU:0, one launch (start us, length us, event | category | flops | bytes accessed | tf_op | source)
XLA Modules:
  0.0 26.3 jit_solution(2019470369431710402)
XLA Ops:
  0.6 0.0 copy-start
  0.6 0.7 %copy-done = f32[2048]{0:T(1024)S(1)} copy-done((f32[2048]{0:T(1024)S(1)}, f32[2048]{0:T(1024)}, u32[]{:S(2)}) %copy-start) | copy-done | bytes 8216
  1.3 23.9 %shard_map.50 = (bf16[4,32,2,2048]{3,2,1,0:T(2,128)(2,1)S(1)}, f32[32,32]{1,0:T(8,128)S(1)}) custom-call(f32[128,2048]{1,0:T(8,128)} %p_ref.1, f32[128,2048]{1,0:T(8,128)} %f_ref.1, f32[1,2048]{1,0:T(1,128)S(1)} %bitcast.4), custom_call_target="tpu_custom_call" | custom-call | tf_op jit(solution)/shard_map/pallas_call | solution.py:258
  25.3 1.0 %shard_map.51 = (bf16[4,32,2,2048]{3,2,1,0:T(2,128)(2,1)}, f32[32,32]{1,0:T(8,128)}) custom-call(bf16[4,32,2,2048]{3,2,1,0:T(2,128)(2,1)S(1)} %get-tuple-element.6.spec_ref, f32[32,32]{1,0:T(8,128)S(1)} %get-tuple-element.7.csd_ref), custom_call_target="tpu_custom_call" | custom-call | tf_op jit(solution)/shard_map/pallas_call | solution.py:285
Async XLA Ops:
  0.6 0.7 %copy-start = (f32[2048]{0:T(1024)S(1)}, f32[2048]{0:T(1024)}, u32[]{:S(2)}) copy-start(f32[2048]{0:T(1024)} %param.5) | copy-start | bytes 24580

commit v4 on v3

--- a/solution.py
+++ b/solution.py
@@ -11,6 +11,7 @@
 HOP = 128
 LANES = 128
 CHUNKS = 8
+AHEAD = 3
 MESH = pl.DeviceIdType.MESH
 
 
@@ -120,7 +121,7 @@
     pl.loop(2, CHUNKS)(prepare)
     for which in range(3):
         sum_copy(which, q).start()
-    for c in range(2, CHUNKS):
+    for c in range(2, AHEAD):
         share(c)
 
     @pl.loop(0, CHUNKS)
@@ -181,10 +182,16 @@
         relay_copy(c, diagonal).wait_recv()
 
     receive(0)
+    share(AHEAD)
 
     @pl.loop(1, CHUNKS)
     def _(c):
         receive(c)
+
+        @pl.when(c + AHEAD < CHUNKS)
+        def _():
+            share(c + AHEAD)
+
         receive_relayed(c - 1)
         for b, value in coefficients(c - 1, 0, 2 * half):
             keep(b, value[:half])

time: 26.5 us -> 27.7 us (1.045)
  Pallas kernels: 24.9 us -> 26.2 us
    pallas_call x1, Pallas kernels: 23.9 us -> 25.2 us  [local(): pl.pallas_call(functools.partial(kernel, n_space, n_blk, float(points * n...]
where the time goes in v4:
time: 27.7 us; the launch traced here: 27.5 us
  Pallas kernels  26.2 us (95%)
  local copies, waits for them, and re-layouts  0.69 us (2%)
  between operations  0.65 us (2%)
    pallas_call x1, Pallas kernels, local(): pl.pallas_call(functools.partial(kernel, n_space, n_blk, float(points * n...  25.2 us
    pallas_call x1, Pallas kernels, local(): pl.pallas_call(finish, out_shape=(jax.ShapeDtypeStruct(spectra.shape, spe...  0.99 us
    unnamed x2, local copies, waits for them, and re-layouts  0.69 us

profile of v4, /device:TPU:0, one launch (start us, length us, event | category | flops | bytes accessed | tf_op | source)
XLA Modules:
  0.0 27.5 jit_solution(5659455945882133543)
XLA Ops:
  0.6 0.0 copy-start
  0.6 0.7 %copy-done = f32[2048]{0:T(1024)S(1)} copy-done((f32[2048]{0:T(1024)S(1)}, f32[2048]{0:T(1024)}, u32[]{:S(2)}) %copy-start) | copy-done | bytes 8216
  1.3 25.2 %shard_map.50 = (bf16[4,32,2,2048]{3,2,1,0:T(2,128)(2,1)S(1)}, f32[32,32]{1,0:T(8,128)S(1)}) custom-call(f32[128,2048]{1,0:T(8,128)} %p_ref.1, f32[128,2048]{1,0:T(8,128)} %f_ref.1, f32[1,2048]{1,0:T(1,128)S(1)} %bitcast.4), custom_call_target="tpu_custom_call" | custom-call | tf_op jit(solution)/shard_map/pallas_call | solution.py:265
  26.5 1.0 %shard_map.51 = (bf16[4,32,2,2048]{3,2,1,0:T(2,128)(2,1)}, f32[32,32]{1,0:T(8,128)}) custom-call(bf16[4,32,2,2048]{3,2,1,0:T(2,128)(2,1)S(1)} %get-tuple-element.6.spec_ref, f32[32,32]{1,0:T(8,128)S(1)} %get-tuple-element.7.csd_ref), custom_call_target="tpu_custom_call" | custom-call | tf_op jit(solution)/shard_map/pallas_call | solution.py:292
Async XLA Ops:
  0.6 0.7 %copy-start = (f32[2048]{0:T(1024)S(1)}, f32[2048]{0:T(1024)}, u32[]{:S(2)}) copy-start(f32[2048]{0:T(1024)} %param.5) | copy-start | bytes 24580

commit v5 on v3

--- a/solution.py
+++ b/solution.py
@@ -10,7 +10,7 @@
 
 HOP = 128
 LANES = 128
-CHUNKS = 8
+CHUNKS = 16
 MESH = pl.DeviceIdType.MESH
 
 

time: 26.5 us -> 28.1 us (1.060)
  Pallas kernels: 24.9 us -> 26.5 us
    pallas_call x1, Pallas kernels: 23.9 us -> 25.5 us  [local(): pl.pallas_call(functools.partial(kernel, n_space, n_blk, float(points * n...]
where the time goes in v5:
time: 28.1 us; the launch traced here: 27.9 us
  Pallas kernels  26.5 us (94%)
  local copies, waits for them, and re-layouts  0.69 us (2%)
  between operations  0.65 us (2%)
    pallas_call x1, Pallas kernels, local(): pl.pallas_call(functools.partial(kernel, n_space, n_blk, float(points * n...  25.5 us
    pallas_call x1, Pallas kernels, local(): pl.pallas_call(finish, out_shape=(jax.ShapeDtypeStruct(spectra.shape, spe...  0.99 us
    unnamed x2, local copies, waits for them, and re-layouts  0.69 us

profile of v5, /device:TPU:0, one launch (start us, length us, event | category | flops | bytes accessed | tf_op | source)
XLA Modules:
  0.0 27.9 jit_solution(2759401682560377864)
XLA Ops:
  0.6 0.0 copy-start
  0.6 0.7 %copy-done = f32[2048]{0:T(1024)S(1)} copy-done((f32[2048]{0:T(1024)S(1)}, f32[2048]{0:T(1024)}, u32[]{:S(2)}) %copy-start) | copy-done | bytes 8216
  1.3 25.5 %shard_map.50 = (bf16[4,32,2,2048]{3,2,1,0:T(2,128)(2,1)S(1)}, f32[32,32]{1,0:T(8,128)S(1)}) custom-call(f32[128,2048]{1,0:T(8,128)} %p_ref.1, f32[128,2048]{1,0:T(8,128)} %f_ref.1, f32[1,2048]{1,0:T(1,128)S(1)} %bitcast.4), custom_call_target="tpu_custom_call" | custom-call | tf_op jit(solution)/shard_map/pallas_call | solution.py:258
  26.9 1.0 %shard_map.51 = (bf16[4,32,2,2048]{3,2,1,0:T(2,128)(2,1)}, f32[32,32]{1,0:T(8,128)}) custom-call(bf16[4,32,2,2048]{3,2,1,0:T(2,128)(2,1)S(1)} %get-tuple-element.6.spec_ref, f32[32,32]{1,0:T(8,128)S(1)} %get-tuple-element.7.csd_ref), custom_call_target="tpu_custom_call" | custom-call | tf_op jit(solution)/shard_map/pallas_call | solution.py:285
Async XLA Ops:
  0.6 0.7 %copy-start = (f32[2048]{0:T(1024)S(1)}, f32[2048]{0:T(1024)}, u32[]{:S(2)}) copy-start(f32[2048]{0:T(1024)} %param.5) | copy-start | bytes 24580

commit v6 on v5

--- a/solution.py
+++ b/solution.py
@@ -10,7 +10,7 @@
 
 HOP = 128
 LANES = 128
-CHUNKS = 16
+CHUNKS = 4
 MESH = pl.DeviceIdType.MESH
 
 

time: 28.1 us -> 26.6 us (0.947)
  Pallas kernels: 26.5 us -> 25 us
    pallas_call x1, Pallas kernels: 25.5 us -> 24 us  [local(): pl.pallas_call(functools.partial(kernel, n_space, n_blk, float(points * n...]
where the time goes in v6:
time: 26.6 us; the launch traced here: 26.4 us
  Pallas kernels  25 us (94%)
  local copies, waits for them, and re-layouts  0.69 us (3%)
  between operations  0.65 us (2%)
    pallas_call x1, Pallas kernels, local(): pl.pallas_call(functools.partial(kernel, n_space, n_blk, float(points * n...  24 us
    pallas_call x1, Pallas kernels, local(): pl.pallas_call(finish, out_shape=(jax.ShapeDtypeStruct(spectra.shape, spe...  0.99 us
    unnamed x2, local copies, waits for them, and re-layouts  0.69 us

profile of v6, /device:TPU:0, one launch (start us, length us, event | category | flops | bytes accessed | tf_op | source)
XLA Modules:
  0.0 26.4 jit_solution(13459846655065172309)
XLA Ops:
  0.6 0.0 copy-start
  0.6 0.7 %copy-done = f32[2048]{0:T(1024)S(1)} copy-done((f32[2048]{0:T(1024)S(1)}, f32[2048]{0:T(1024)}, u32[]{:S(2)}) %copy-start) | copy-done | bytes 8216
  1.3 24.0 %shard_map.50 = (bf16[4,32,2,2048]{3,2,1,0:T(2,128)(2,1)S(1)}, f32[32,32]{1,0:T(8,128)S(1)}) custom-call(f32[128,2048]{1,0:T(8,128)} %p_ref.1, f32[128,2048]{1,0:T(8,128)} %f_ref.1, f32[1,2048]{1,0:T(1,128)S(1)} %bitcast.4), custom_call_target="tpu_custom_call" | custom-call | tf_op jit(solution)/shard_map/pallas_call | solution.py:258
  25.4 1.0 %shard_map.51 = (bf16[4,32,2,2048]{3,2,1,0:T(2,128)(2,1)}, f32[32,32]{1,0:T(8,128)}) custom-call(bf16[4,32,2,2048]{3,2,1,0:T(2,128)(2,1)S(1)} %get-tuple-element.6.spec_ref, f32[32,32]{1,0:T(8,128)S(1)} %get-tuple-element.7.csd_ref), custom_call_target="tpu_custom_call" | custom-call | tf_op jit(solution)/shard_map/pallas_call | solution.py:285
Async XLA Ops:
  0.6 0.7 %copy-start = (f32[2048]{0:T(1024)S(1)}, f32[2048]{0:T(1024)}, u32[]{:S(2)}) copy-start(f32[2048]{0:T(1024)} %param.5) | copy-start | bytes 24580
